TPU v7x, 32 devices: a whole 2x2x4 slice. The times are simulated.
32 devices in a mesh: section: 2 (over x), dp: 4 (over z), tensor: 4 (over y, core).
Axes of the slice: x: 2, y: 2, z: 4, core: 2. Of those that a mesh axis runs over, the one named last changes fastest.
Arguments:
- queries: bfloat16 [2, 1024, 8192], P('section', 'dp', 'tensor'), may hold values from -256 to 256
- image: bfloat16 [8192, 512], P(('section', 'tensor'), 'dp'), may hold values from -6 to 6
- w_key: bfloat16 [2, 8192, 1024], P('section', None, 'tensor'), may hold values from -0.0625 to 0.0625
- w_value: bfloat16 [2, 8192, 1024], P('section', None, 'tensor'), may hold values from -0.0625 to 0.0625
- gates: float32 [2], P('section'), may hold values from 0.3 to 1.5
- tiles: int32 [4], P('dp'), may hold values from 1 to 4, as said below
- cotangent: bfloat16 [2, 1024, 8192], P('section', 'dp', 'tensor'), may hold values from -6 to 6
Outputs:
- attended: bfloat16 [2, 1024, 8192], P('section', 'dp', 'tensor')
- d_queries: bfloat16 [2, 1024, 8192], P('section', 'dp', 'tensor')
- d_image: bfloat16 [8192, 512], P(('section', 'tensor'), 'dp')
Inputs may be any that keep to these rules, and one draw needn't show every extreme that they name: The first tiles[b] * 32 image tokens are valid for sample b; some sample has 4 tiles and some has one.
All inputs are finite; a program needn't handle non-finite values.
Results may differ from a plain program's by a relative error of at most 0.013.
The roundings to bfloat16 on the way count: a program that leaves them out, or rounds other values in their place, can miss the bound.
Values may be sent and summed in bfloat16 or wider, within the bound.
A program may use at most 64 MiB of HBM per device.

v0:
```python
import math

import jax
import jax.numpy as jnp
from jax import lax
from jax.sharding import PartitionSpec as P

HD = 128
TILE_TOK = 32


def shards(queries, image, w_key, w_value, gates, tiles, cotangent):
    weight_key = w_key[0]
    weight_value = w_value[0]
    width = weight_key.shape[1]
    img_count = image.shape[1]
    piece = lax.all_gather(image, ("section", "tensor"), axis=0, tiled=True)
    rows_key = weight_key
    rows_value = weight_value
    dims = (((0,), (0,)), ((), ()))
    part_key = lax.dot_general(piece, rows_key, dims, preferred_element_type=jnp.float32)
    part_value = lax.dot_general(piece, rows_value, dims, preferred_element_type=jnp.float32)
    key_rows = part_key.astype(jnp.bfloat16)
    value_rows = part_value.astype(jnp.bfloat16)
    text = queries[0]
    upstream = cotangent[0]
    tokens = text.shape[0]
    kv_count = width // HD
    q_count = text.shape[1] // HD
    group = q_count // kv_count
    query_heads = text.reshape(tokens, kv_count, group, HD)
    key_heads = key_rows.reshape(img_count, kv_count, HD)
    value_heads = value_rows.reshape(img_count, kv_count, HD)
    scores = jnp.einsum(
        "tkgd,skd->kgts", query_heads, key_heads, preferred_element_type=jnp.float32
    ) / math.sqrt(HD)
    allowed = jnp.arange(img_count) < tiles[0] * TILE_TOK
    scores = jnp.where(allowed, scores, jnp.float32(-1e30))
    top = jnp.max(scores, axis=-1, keepdims=True)
    expo = jnp.exp(scores - top)
    probs = expo / jnp.sum(expo, axis=-1, keepdims=True)
    probs_b = probs.astype(jnp.bfloat16)
    context = jnp.einsum("kgts,skd->tkgd", probs_b, value_heads, preferred_element_type=jnp.float32)
    scale = jnp.tanh(gates[0])
    attended = (scale * context).reshape(tokens, q_count * HD).astype(jnp.bfloat16)
    d_context = (scale * upstream.astype(jnp.float32)).astype(jnp.bfloat16)
    d_context = d_context.reshape(tokens, kv_count, group, HD)
    d_values = jnp.einsum(
        "kgts,tkgd->skd", probs_b, d_context, preferred_element_type=jnp.float32
    ).astype(jnp.bfloat16)
    d_probs = jnp.einsum(
        "tkgd,skd->kgts", d_context, value_heads, preferred_element_type=jnp.float32
    )
    delta = jnp.sum(probs * d_probs, axis=-1, keepdims=True)
    d_scores = (probs * (d_probs - delta) / math.sqrt(HD)).astype(jnp.bfloat16)
    d_query = jnp.einsum("kgts,skd->tkgd", d_scores, key_heads, preferred_element_type=jnp.float32)
    d_query = d_query.reshape(tokens, q_count * HD).astype(jnp.bfloat16)
    d_keys = jnp.einsum(
        "kgts,tkgd->skd", d_scores, query_heads, preferred_element_type=jnp.float32
    ).astype(jnp.bfloat16)
    d_keys = d_keys.reshape(img_count, width)
    d_values = d_values.reshape(img_count, width)
    rows_key = weight_key
    rows_value = weight_value
    dims = (((1,), (1,)), ((), ()))
    term = lax.dot_general(rows_key, d_keys, dims, preferred_element_type=jnp.float32)
    grad_rows = lax.psum_scatter(
        term + lax.dot_general(rows_value, d_values, dims, preferred_element_type=jnp.float32),
        ("section", "tensor"),
        scatter_dimension=0,
        tiled=True,
    )
    return (attended[None], d_query[None], grad_rows.astype(jnp.bfloat16))


def solution(mesh):
    return jax.shard_map(
        shards,
        mesh=mesh,
        in_specs=(
            P("section", "dp", "tensor"),
            P(("section", "tensor"), "dp"),
            P("section", None, "tensor"),
            P("section", None, "tensor"),
            P("section"),
            P("dp"),
            P("section", "dp", "tensor"),
        ),
        out_specs=(
            P("section", "dp", "tensor"),
            P("section", "dp", "tensor"),
            P(("section", "tensor"), "dp"),
        ),
        check_vma=False,
    )
```

profile of v0, /device:TPU:0, one launch (start us, length us, event | category | flops | bytes accessed | tf_op | source)
XLA Modules:
  0.0 127.1 jit_solution(7864442530545022674)
XLA Ops:
  7.2 0.0 copy-start.3
  7.2 0.0 all-gather.2.cloned.1.call-start
  7.2 0.7 all-gather.2.cloned.1.call-update
  7.9 0.0 reduce-scatter.2.cloned.1.call-start
  9.3 2.3 %copy.44 = bf16[1,256,2048]{1,2,0:T(8,128)(2,1)} copy(bf16[1,256,2048]{2,1,0:T(8,128)(2,1)} %param.7) | data formatting | bytes 2097152 | tf_op jit(solution)/shard_map/reshape;squeeze | solution.py:31
  11.6 0.0 copy-done.3
  11.6 0.3 fusion.25
  11.9 0.2 copy.45
  12.1 28.4 %all-gather.2.cloned.1.call-done = bf16[8192,128]{1,0:T(8,128)(2,1)} async-done(((bf16[1024,128]{1,0:T(8,128)(2,1)}), bf16[8192,128]{1,0:T(8,128)(2,1)}) %all-gather.2.cloned.1.call-update) | async-done | bytes 2097168 | tf_op jit(solution)/shard_map/all_gather | solution.py:17
  40.5 3.9 %fusion.19 = bf16[128,256]{1,0:T(8,128)(2,1)S(1)} fusion(bf16[8192,128]{1,0:T(8,128)(2,1)} %all-gather.2.cloned.1.call-done, bf16[1,8192,256]{2,1,0:T(8,128)(2,1)} %param.10), kind=kOutput, calls=%fused_computation.28 | convolution fusion | flops 536903680 | bytes 6356992 | tf_op jit(solution)/shard_map/dot_general | solution.py:22
  44.5 3.2 %fusion.22 = bf16[128,256]{1,0:T(8,128)(2,1)S(1)} fusion(bf16[8192,128]{1,0:T(8,128)(2,1)S(1)} %copy-done.2, bf16[1,8192,256]{2,1,0:T(8,128)(2,1)} %param.9), kind=kOutput, calls=%fused_computation.29 | convolution fusion | flops 536903680 | bytes 6356992 | tf_op jit(solution)/shard_map/dot_general | solution.py:21
  47.7 0.0 copy-start.4
  47.7 0.1 copy.29
  47.9 1.8 %fusion.26 = f32[2,128,256,8]{2,1,3,0:T(8,128)} fusion(bf16[256,2,8,128]{3,2,1,0:T(8,128)(2,1)S(1)} %bitcast.92, bf16[128,2,128,1]{2,1,0,3:T(2,128)(2,1)S(1)} %bitcast.98), kind=kOutput, calls=%fused_computation.31 | convolution fusion | flops 134217728 | bytes 3211264 | tf_op jit(solution)/shard_map/tkgd,skd->kgts/dot_general | solution.py:51
  49.7 2.2 %fusion.43 = (f32[2,8,256]{2,1,0:T(8,128)S(1)}, f32[2,8,256,128]{2,3,1,0:T(8,128)}) fusion(pred[128]{0:T(512)(128)(4,1)S(1)} %iota_compare_fusion, bf16[128,2,128,1]{0,2,3,1:T(8,128)(2,1)S(1)} %copy.29, bf16[256,2,8,128]{0,3,2,1:T(8,128)(2,1)S(1)} %bitcast.95), kind=kOutput, calls=%fused_computation.49 | convolution fusion | flops 136315008 | bytes 3227776 | tf_op jit(solution)/shard_map/sub | solution.py:40
  51.8 1.8 %fusion.42 = bf16[2,8,256,128]{2,3,1,0:T(8,128)(2,1)S(1)} fusion(f32[2,8,256,128]{2,3,1,0:T(8,128)} %get-tuple-element.7, f32[2,8,256]{2,1,0:T(8,128)S(1)} %get-tuple-element.6), kind=kLoop, calls=%fused_computation.48 | loop fusion | flops 1048576 | bytes 3162112 | tf_op jit(solution)/shard_map/convert_element_type | solution.py:42
  53.6 4.3 %fusion.17 = bf16[2,128,128]{1,2,0:T(8,128)(2,1)S(1)} fusion(bf16[256,2,8,128]{0,3,2,1:T(8,128)(2,1)S(1)} %bitcast.96, f32[2,128,256,8]{2,1,3,0:T(8,128)} %fusion.26, f32[2,8,256,128]{2,3,1,0:T(8,128)} %get-tuple-element.7, f32[2,8,256]{2,1,0:T(8,128)S(1)} %get-tuple-element.6), kind=kOutput, calls=%fused_computation.26 | convolution fusion | flops 137924736 | bytes 5324800 | tf_op jit(solution)/shard_map/kgts,tkgd->skd/dot_general | solution.py:58
  58.0 1.1 copy.34
  59.1 0.0 copy-start.1
  59.1 0.5 fusion.18
  59.6 1.7 %copy-done.1 = bf16[1,8192,256]{2,1,0:T(8,128)(2,1)S(1)} copy-done((bf16[1,8192,256]{2,1,0:T(8,128)(2,1)S(1)}, bf16[1,8192,256]{2,1,0:T(8,128)(2,1)}, u32[]{:S(2)}) %copy-start.1) | copy-done | bytes 4194328
  61.3 1.5 %fusion.3 = f32[128,8192]{1,0:T(8,128)S(1)} fusion(bf16[128,256]{0,1:T(8,128)(2,1)S(1)} %bitcast.101, bf16[1,8192,256]{2,1,0:T(8,128)(2,1)S(1)} %copy-done.1), kind=kOutput, calls=%fused_computation.4 | convolution fusion | flops 536870912 | bytes 8454144 | tf_op jit(solution)/shard_map/dot_general | solution.py:66
  62.8 0.7 copy-done
  63.4 3.4 %fusion.2 = f32[8192,128]{0,1:T(8,128)} fusion(f32[128,8192]{1,0:T(8,128)S(1)} %fusion.3, bf16[128,256]{0,1:T(8,128)(2,1)S(1)} %bitcast.102, bf16[1,8192,256]{2,1,0:T(8,128)(2,1)S(1)} %copy-done), kind=kOutput, calls=%fused_computation.3 | convolution fusion | flops 537919488 | bytes 12648448 | tf_op jit(solution)/shard_map/dot_general | solution.py:68
  66.9 0.0 reduce-scatter.2.cloned.1.call-update
  66.9 4.3 %convolution_convert_fusion = bf16[2,128,8,256]{3,1,2,0:T(8,128)(2,1)S(1)} fusion(bf16[128,2,128,1]{0,2,3,1:T(8,128)(2,1)S(1)} %copy.29, f32[2,128,256,8]{2,1,3,0:T(8,128)} %fusion.26, f32[2,8,256,128]{2,3,1,0:T(8,128)} %get-tuple-element.7, f32[2,8,256]{2,1,0:T(8,128)S(1)} %get-tuple-element.6), kind=kOutput, calls=%fused_computation.23 | convolution fusion | flops 138416256 | bytes 5324800 | tf_op jit(solution)/shard_map/kgts,skd->tkgd/dot_general | solution.py:56
  71.2 1.4 %copy.23 = bf16[1,256,2048]{2,1,0:T(8,128)(2,1)} copy(bf16[1,256,2048]{1,2,0:T(8,128)(2,1)S(1)} %bitcast.97) | data formatting | bytes 2097152
  72.7 0.5 multiply_convert_fusion.1
  73.2 1.4 %copy.22 = bf16[1,256,2048]{2,1,0:T(8,128)(2,1)} copy(bf16[1,256,2048]{1,2,0:T(8,128)(2,1)S(1)} %bitcast.94) | data formatting | bytes 2097152
  74.6 43.8 %reduce-scatter.2.cloned.1.call-done = f32[1024,128]{0,1:T(8,128)} async-done(((f32[8192,128]{0,1:T(8,128)}), f32[1024,128]{0,1:T(8,128)}) %reduce-scatter.2.cloned.1.call-update) | async-done | bytes 524304 | tf_op jit(solution)/shard_map/reduce_scatter | solution.py:67
  118.4 1.1 convert_element_type.88
  119.4 0.8 copy.24
  (7 shorter events, 0.1 us)
Async XLA Ops:
  7.2 4.4 %copy-start.3 = (bf16[1,256,2048]{2,1,0:T(8,128)(2,1)S(1)}, bf16[1,256,2048]{2,1,0:T(8,128)(2,1)}, u32[]{:S(2)}) copy-start(bf16[1,256,2048]{2,1,0:T(8,128)(2,1)} %param.13) | copy-start | bytes 3145732
  7.2 33.4 %all-gather.2.cloned.1.call-start = ((), (), s32[]{:S(2)}) async-start(), calls=%async_computation.1 | async-start | bytes 2359296 | tf_op jit(solution)/shard_map/all_gather | solution.py:17
  7.9 110.5 %reduce-scatter.2.cloned.1.call-start = ((), (), s32[]{:S(2)}) async-start(), calls=%async_computation.2 | async-start | bytes 4718592 | tf_op jit(solution)/shard_map/reduce_scatter | solution.py:67
  40.5 4.0 %copy-start.2 = (bf16[8192,128]{1,0:T(8,128)(2,1)S(1)}, bf16[8192,128]{1,0:T(8,128)(2,1)}, u32[]{:S(2)}) copy-start(bf16[8192,128]{1,0:T(8,128)(2,1)} %all-gather.2.cloned.1.call-done) | copy-start | bytes 6291460
  47.7 2.0 %copy-start.4 = (bf16[1,256,2048]{1,2,0:T(8,128)(2,1)S(1)}, bf16[1,256,2048]{1,2,0:T(8,128)(2,1)}, u32[]{:S(2)}) copy-start(bf16[1,256,2048]{1,2,0:T(8,128)(2,1)} %copy.44) | copy-start | bytes 3145732
  59.1 2.2 %copy-start.1 = (bf16[1,8192,256]{2,1,0:T(8,128)(2,1)S(1)}, bf16[1,8192,256]{2,1,0:T(8,128)(2,1)}, u32[]{:S(2)}) copy-start(bf16[1,8192,256]{2,1,0:T(8,128)(2,1)} %param.9) | copy-start | bytes 12582916
  61.3 2.2 %copy-start = (bf16[1,8192,256]{2,1,0:T(8,128)(2,1)S(1)}, bf16[1,8192,256]{2,1,0:T(8,128)(2,1)}, u32[]{:S(2)}) copy-start(bf16[1,8192,256]{2,1,0:T(8,128)(2,1)} %param.10) | copy-start | bytes 12582916
Sparse Core Ops, SparseCore 0:
  9.9 30.5 all-gather.1
  67.0 51.3 reduce-scatter.1
where the time goes:
time: 127 us
  waiting for transfers between devices  72.9 us (57%)
  matrix products  25.6 us (20%)
  between operations  15.5 us (12%)
  local copies, waits for them, and re-layouts  9.82 us (8%)
  other arithmetic  3.17 us (2%)
    reduce_scatter x1, waiting for transfers between devices, shards(): lax.psum_scatter(term + lax.dot_general(rows_value, d_values, dims, prefe...  43.8 us
    all_gather x1, waiting for transfers between devices, shards(): piece = lax.all_gather(image, ('section', 'tensor'), axis=0, tiled=True)  28.4 us
    unnamed x14, local copies, waits for them, and re-layouts  6.32 us
    dot_general x1, matrix products, shards(): jnp.einsum('kgts,skd->tkgd', d_scores, key_heads, preferred_element_type=...  4.35 us
    dot_general x1, matrix products, shards(): jnp.einsum('kgts,tkgd->skd', d_scores, query_heads, preferred_element_typ...  4.32 us
    dot_general x1, matrix products, shards(): lax.dot_general(piece, rows_value, dims, preferred_element_type=jnp.float32)  3.94 us
    dot_general x1, matrix products, shards(): lax.dot_general(rows_value, d_values, dims, preferred_element_type=jnp.fl...  3.43 us
    dot_general x1, matrix products, shards(): lax.dot_general(piece, rows_key, dims, preferred_element_type=jnp.float32)  3.17 us
  transfers between devices with their start and end apart: 2, of which 2 were waited for; matrix products, arithmetic and copies ran while one was open for 8% of the time, Pallas kernels for 0%

commit v1 on v0

v1 whole, which is shorter than its diff:
```python
import functools
import math

import jax
import jax.numpy as jnp
from jax import lax
from jax.experimental import pallas as pl
from jax.experimental.pallas import tpu as pltpu
from jax.sharding import PartitionSpec as P

HD = 128
TILE_TOK = 32
CORES = 2
MESH = pl.DeviceIdType.MESH
F32 = jnp.float32
BF16 = jnp.bfloat16
NT = (((1,), (1,)), ((), ()))
TN = (((0,), (0,)), ((), ()))
NN = (((1,), (0,)), ((), ()))


def dot(a, b, dims):
    return lax.dot_general(a, b, dims, preferred_element_type=F32)


def counts(n_s, n_y):
    near = (n_s - 1) + (n_y - 1)
    far = (n_s - 1) * (n_y - 1)
    chips = n_s * n_y
    gather_sends = 2 * near + 2 * far + 2 * chips
    scatter_sends = chips + 2 * far + 2 * near
    return gather_sends + scatter_sends


def kernel(
    n_s, n_y, block,
    gates_ref, tiles_ref, q_hbm, img_hbm, wk_hbm, wv_hbm, cot_hbm,
    att_hbm, dq_hbm, dimg_ref,
    wk, wv, q, cot, att, dq, img, acc, kv, dk, dv, dkv_t, probs_t, ds_t,
    pair_out, pair_in, held, out_send, mid, last,
    local_sem, send_sem, img_sem, pair_sem, mid_sem, last_sem,
):
    s = lax.axis_index("section")
    t = lax.axis_index("tensor")
    y = t // CORES
    c = t % CORES
    n_t = n_y * CORES
    chunk = img_hbm.shape[0]
    half = chunk // 2
    slots = img_hbm.shape[1]
    width = wk.shape[1]
    tokens, columns = q.shape
    heads = columns // HD
    group = columns // width
    far = [(ds, dy) for ds in range(1, n_s) for dy in range(1, n_y)]
    near_s = [(ds, 0) for ds in range(1, n_s)]
    near_y = [(0, dy) for dy in range(1, n_y)]

    def place(ds, dy):
        return ds * n_y + dy

    def to(ds, dy, other=False):
        core = 1 - c if other else c
        return {
            "section": lax.rem(s + ds, n_s),
            "tensor": lax.rem(y + dy, n_y) * CORES + core,
        }

    def rows_of(ds, dy, core):
        chip = lax.rem(s + ds + n_s, n_s) * n_t + lax.rem(y + dy + n_y, n_y) * CORES
        return pl.ds(pl.multiple_of((chip + core) * chunk, chunk), chunk)

    sent = []

    def send(src, dst, sem, device):
        copy = pltpu.make_async_remote_copy(
            src_ref=src, dst_ref=dst, send_sem=send_sem.at[len(sent)],
            recv_sem=sem, device_id=device, device_id_type=MESH,
        )
        copy.start()
        sent.append(copy)

    def arrive(dst, sem):
        pltpu.make_async_remote_copy(
            src_ref=dst, dst_ref=dst, send_sem=send_sem.at[0],
            recv_sem=sem, device_id=to(0, 0, True), device_id_type=MESH,
        ).wait_recv()

    local = []

    def bring(src, dst):
        copy = pltpu.make_async_copy(src, dst, local_sem.at[len(local)])
        copy.start()
        local.append(copy)
        return copy

    barrier = pltpu.get_barrier_semaphore()
    partners = [to(0, 0, True)] + [to(ds, dy) for ds, dy in near_s + near_y]
    for device in partners:
        pl.semaphore_signal(barrier, inc=1, device_id=device, device_id_type=MESH)
    own = bring(img_hbm, img.at[0, 0])
    parts = 4
    depth = wk.shape[0] // parts
    weights = []
    for i in range(parts):
        piece = pl.ds(i * depth, depth)
        weights.append(bring(wk_hbm.at[piece], wk.at[piece]))
        weights.append(bring(wv_hbm.at[piece], wv.at[piece]))
    text = [bring(q_hbm, q), bring(cot_hbm, cot)]
    pl.semaphore_wait(barrier, len(partners))

    def piece_of(ds, dy, core, h):
        return img.at[place(ds, dy), core, pl.ds(h * half, half)]

    def own_piece(h):
        return img_hbm.at[pl.ds(h * half, half)]

    for h in range(2):
        for ds, dy in near_s:
            send(own_piece(h), piece_of(ds, dy, 0, h), img_sem.at[place(ds, dy), 0, h], to(ds, dy))
        for ds, dy in near_y:
            send(own_piece(1 - h), piece_of(ds, dy, 0, 1 - h), img_sem.at[place(ds, dy), 0, 1 - h], to(ds, dy))
    for h in range(2):
        send(own_piece(h), piece_of(0, 0, 1, h), img_sem.at[0, 1, h], to(0, 0, True))

    def receive(ds, dy, core, h):
        arrive(piece_of(ds, dy, core, h), img_sem.at[place(ds, dy), core, h])

    def share(ds, dy, h):
        send(piece_of(ds, dy, 0, h), piece_of(ds, dy, 1, h), img_sem.at[place(ds, dy), 1, h], to(0, 0, True))

    def project(ds, dy, core):
        rows = rows_of(-ds, -dy, 1 - c if core else c)
        features = img[place(ds, dy), core]
        acc[:, :width] += dot(features, wk[rows, :], TN)
        acc[:, width:] += dot(features, wv[rows, :], TN)

    for ds, dy in near_s:
        receive(ds, dy, 0, 0)
        for _, ey in near_y:
            send(piece_of(ds, 0, 0, 0), piece_of(ds, ey, 0, 0), img_sem.at[place(ds, ey), 0, 0], to(0, ey))
        share(ds, dy, 0)
    for ds, dy in near_y:
        receive(ds, dy, 0, 1)
        for es, _ in near_s:
            send(piece_of(0, dy, 0, 1), piece_of(es, dy, 0, 1), img_sem.at[place(es, dy), 0, 1], to(es, 0))
        share(ds, dy, 1)
    acc[...] = jnp.zeros_like(acc)
    for copy in weights:
        copy.wait()
    own.wait()
    project(0, 0, 0)
    for h in range(2):
        receive(0, 0, 1, h)
    project(0, 0, 1)
    for ds, dy in near_s:
        receive(ds, dy, 0, 1)
        share(ds, dy, 1)
    for ds, dy in near_y:
        receive(ds, dy, 0, 0)
        share(ds, dy, 0)
    for ds, dy in near_s + near_y:
        project(ds, dy, 0)
    for ds, dy in near_s + near_y:
        for h in range(2):
            receive(ds, dy, 1, h)
        project(ds, dy, 1)
    for ds, dy in far:
        for h in range(2):
            receive(ds, dy, 0, h)
            share(ds, dy, h)
        project(ds, dy, 0)
    for ds, dy in far:
        for h in range(2):
            receive(ds, dy, 1, h)
        project(ds, dy, 1)

    kv[...] = acc[...].astype(BF16)
    dk[...] = jnp.zeros_like(dk)
    dv[...] = jnp.zeros_like(dv)
    for copy in text:
        copy.wait()
    scale = jnp.tanh(jnp.full((1, HD), gates_ref[0], F32))
    valid = tiles_ref[0] * TILE_TOK
    factor = 1.0 / math.sqrt(HD)

    def lanes(i, offset=0):
        return pl.ds(pl.multiple_of(i * HD + offset, HD), HD)

    def attend(b, carry):
        first = b * block
        j = first // group
        key = kv[:, lanes(j)]
        value = kv[:, lanes(j, width)]
        allowed = lax.broadcasted_iota(jnp.int32, (slots, tokens), 0) < valid
        total_k = dk[:, lanes(j)]
        total_v = dv[:, lanes(j)]
        for i in range(block):
            query = q[:, lanes(first + i)]
            upstream = (scale * cot[:, lanes(first + i)].astype(F32)).astype(BF16)
            scores = jnp.where(allowed, dot(key, query, NT) * factor, -1e30)
            expo = jnp.exp(scores - jnp.max(scores, axis=0, keepdims=True))
            probs = expo * (1.0 / jnp.sum(expo, axis=0, keepdims=True))
            probs_b = probs.astype(BF16)
            d_probs = dot(value, upstream, NT)
            delta = jnp.sum(probs * d_probs, axis=0, keepdims=True)
            d_scores = (probs * (d_probs - delta) * factor).astype(BF16)
            total_v += dot(probs_b, upstream, NN)
            total_k += dot(d_scores, query, NN)
            probs_t[first + i] = probs_b
            ds_t[first + i] = d_scores
        dk[:, lanes(j)] = total_k
        dv[:, lanes(j)] = total_v
        return carry

    lax.fori_loop(0, heads // block, attend, 0)
    dkv_t[:width, :] = dk[...].astype(BF16).T
    dkv_t[width:, :] = dv[...].astype(BF16).T

    def finish(b, carry):
        first = b * block
        j = first // group
        key = kv[:, lanes(j)]
        value = kv[:, lanes(j, width)]
        for i in range(block):
            context = dot(probs_t[first + i], value, TN)
            att[:, lanes(first + i)] = (scale * context).astype(BF16)
            dq[:, lanes(first + i)] = dot(ds_t[first + i], key, TN).astype(BF16)
        return carry

    def term(ds, dy, core):
        rows = rows_of(ds, dy, core)
        return dot(wk[rows, :], dkv_t[:width, :], NN) + dot(wv[rows, :], dkv_t[width:, :], NN)

    def start_pair(ds, dy):
        k = place(ds, dy)
        pair_out[k] = term(ds, dy, 1 - c).astype(BF16)
        send(pair_out.at[k], pair_in.at[k], pair_sem.at[k], to(0, 0, True))
        held[k] = term(ds, dy, c)

    def end_pair(ds, dy):
        k = place(ds, dy)
        arrive(pair_in.at[k], pair_sem.at[k])
        total = held[k] + pair_in[k].astype(F32)
        if (ds, dy) in far:
            out_send[k] = total.astype(BF16)
            send(out_send.at[k, pl.ds(0, half)], mid.at[0, k], mid_sem.at[0, k], to(ds, 0))
            send(out_send.at[k, pl.ds(half, half)], mid.at[1, k], mid_sem.at[1, k], to(0, dy))
        else:
            held[k] = total
            if (ds, dy) != (0, 0):
                h = 0 if ds else 1
                pass_on(ds, dy, h)

    def pass_on(ds, dy, h):
        k = place(ds, dy)
        piece = pl.ds(h * half, half)
        out_send[k, piece] = held[k, piece].astype(BF16)
        send(out_send.at[k, piece], last.at[k, piece], last_sem.at[k, h], to(ds, dy))

    order = far + near_s + near_y + [(0, 0)]
    for n, target in enumerate(order):
        start_pair(*target)
        if n:
            end_pair(*order[n - 1])
    end_pair(*order[-1])
    for ds, dy in near_s + near_y:
        k = place(ds, dy)
        h = 1 if ds else 0
        piece = pl.ds(h * half, half)
        for es, ey in far:
            if (es == ds) if ds else (ey == dy):
                m = place(es, ey)
                arrive(mid.at[h, m], mid_sem.at[h, m])
                held[k, piece] += mid[h, m].astype(F32)
        pass_on(ds, dy, h)
    lax.fori_loop(0, heads // block, finish, 0)
    bring(att, att_hbm)
    bring(dq, dq_hbm)
    total = held[0]
    for ds, dy in near_s + near_y:
        k = place(ds, dy)
        for h in range(2):
            arrive(last.at[k, pl.ds(h * half, half)], last_sem.at[k, h])
        total += last[k].astype(F32)
    dimg_ref[...] = total.astype(BF16)
    for copy in local[-2:]:
        copy.wait()
    for copy in sent:
        copy.wait_send()


def solution(mesh):
    n_s = mesh.shape["section"]
    n_t = mesh.shape["tensor"]
    n_y = n_t // CORES
    chips = n_s * n_y

    def shards(queries, image, w_key, w_value, gates, tiles, cotangent):
        text, upstream = queries[0], cotangent[0]
        weight_key, weight_value = w_key[0], w_value[0]
        tokens, columns = text.shape
        d, width = weight_key.shape
        chunk, slots = image.shape
        heads = columns // HD
        group = columns // width
        block = math.gcd(group, 4)
        half = chunk // 2
        smem = pl.BlockSpec(memory_space=pltpu.SMEM)
        anywhere = pl.BlockSpec(memory_space=pl.ANY)
        vmem = pl.BlockSpec(memory_space=pltpu.VMEM)
        dma = pltpu.SemaphoreType.DMA
        attended, d_query, d_image = pl.pallas_call(
            functools.partial(kernel, n_s, n_y, block),
            out_shape=(
                jax.ShapeDtypeStruct((tokens, columns), BF16),
                jax.ShapeDtypeStruct((tokens, columns), BF16),
                jax.ShapeDtypeStruct((chunk, slots), BF16),
            ),
            in_specs=[smem, smem] + [anywhere] * 5,
            out_specs=(anywhere, anywhere, vmem),
            scratch_shapes=[
                pltpu.VMEM((d, width), BF16),
                pltpu.VMEM((d, width), BF16),
                pltpu.VMEM((tokens, columns), BF16),
                pltpu.VMEM((tokens, columns), BF16),
                pltpu.VMEM((tokens, columns), BF16),
                pltpu.VMEM((tokens, columns), BF16),
                pltpu.VMEM((chips, CORES, chunk, slots), BF16),
                pltpu.VMEM((slots, 2 * width), F32),
                pltpu.VMEM((slots, 2 * width), BF16),
                pltpu.VMEM((slots, width), F32),
                pltpu.VMEM((slots, width), F32),
                pltpu.VMEM((2 * width, slots), BF16),
                pltpu.VMEM((heads, slots, tokens), BF16),
                pltpu.VMEM((heads, slots, tokens), BF16),
                pltpu.VMEM((chips, chunk, slots), BF16),
                pltpu.VMEM((chips, chunk, slots), BF16),
                pltpu.VMEM((chips, chunk, slots), F32),
                pltpu.VMEM((chips, chunk, slots), BF16),
                pltpu.VMEM((2, chips, half, slots), BF16),
                pltpu.VMEM((chips, chunk, slots), BF16),
                dma((13,)),
                dma((counts(n_s, n_y),)),
                dma((chips, CORES, 2)),
                dma((chips,)),
                dma((2, chips)),
                dma((chips, 2)),
            ],
            compiler_params=pltpu.CompilerParams(
                collective_id=0, has_side_effects=True, vmem_limit_bytes=48 * 1024 * 1024
            ),
            cost_estimate=pl.CostEstimate(
                flops=8 * d * width * slots + 12 * tokens * columns * slots,
                bytes_accessed=4 * d * width + 8 * tokens * columns,
                transcendentals=heads * tokens * slots,
            ),
        )(gates, tiles, text, image, weight_key, weight_value, upstream)
        return attended[None], d_query[None], d_image

    return jax.shard_map(
        shards,
        mesh=mesh,
        in_specs=(
            P("section", "dp", "tensor"),
            P(("section", "tensor"), "dp"),
            P("section", None, "tensor"),
            P("section", None, "tensor"),
            P("section"),
            P("dp"),
            P("section", "dp", "tensor"),
        ),
        out_specs=(
            P("section", "dp", "tensor"),
            P("section", "dp", "tensor"),
            P(("section", "tensor"), "dp"),
        ),
        check_vma=False,
    )
```

time: 127 us -> 41.5 us (0.33)
  waiting for transfers between devices: 72.9 us -> 0 us
  Pallas kernels: 0 us -> 33.3 us
  matrix products: 25.6 us -> 0 us
  between operations: 15.5 us -> 1.94 us
  local copies, waits for them, and re-layouts: 9.82 us -> 6.04 us
  other arithmetic: 3.17 us -> 0 us
    reduce_scatter x1 -> x0, waiting for transfers between devices: 43.8 us -> none  [shards(): lax.psum_scatter(term + lax.dot_general(rows_value, d_values, dims, prefe...]
    pallas_call x0 -> x1, Pallas kernels: none -> 33.3 us  [shards(): pl.pallas_call(functools.partial(kernel, n_s, n_y, block), out_shape=(jax...]
    all_gather x1 -> x0, waiting for transfers between devices: 28.4 us -> none  [shards(): piece = lax.all_gather(image, ('section', 'tensor'), axis=0, tiled=True)]
    dot_general x9 -> x0, matrix products: 23.5 us -> none  [the longest x1 4.35 us: shards(): jnp.einsum('kgts,skd->tkgd', d_scores, key_heads, preferred_element_type=...]
    convert_element_type x2 -> x0, other arithmetic: 2.86 us -> none  [the longest x1 1.79 us: shards(): probs_b = probs.astype(jnp.bfloat16)]
    another operation x1 -> x0, local copies, waits for them, and re-layouts: 2.26 us -> none  [shards(): query_heads = text.reshape(tokens, kv_count, group, HD)]
    sub x1 -> x0, matrix products: 2.18 us -> none  [shards(): expo = jnp.exp(scores - top)]
    unnamed x14 -> x9, local copies, waits for them, and re-layouts: 6.32 us -> 6.04 us
  transfers between devices with their start and end apart: 2 -> 0, of which waited for: 2 -> 0; matrix products, arithmetic and copies ran while one was open for 8% -> 0% of each run, Pallas kernels for 0% -> 0%
where the time goes in v1:
time: 41.5 us; the launch traced here: 41.2 us
  Pallas kernels  33.3 us (80%)
  local copies, waits for them, and re-layouts  6.04 us (15%)
  between operations  1.94 us (5%)
    pallas_call x1, Pallas kernels, shards(): pl.pallas_call(functools.partial(kernel, n_s, n_y, block), out_shape=(jax...  33.3 us
    unnamed x9, local copies, waits for them, and re-layouts  6.04 us

profile of v1, /device:TPU:0, one launch (start us, length us, event | category | flops | bytes accessed | tf_op | source)
XLA Modules:
  0.0 41.2 jit_solution(17541442878928837601)
XLA Ops:
  1.9 0.0 copy-start
  1.9 1.2 %copy-done = bf16[1,256,2048]{2,1,0:T(8,128)(2,1)S(1)} copy-done((bf16[1,256,2048]{2,1,0:T(8,128)(2,1)S(1)}, bf16[1,256,2048]{2,1,0:T(8,128)(2,1)}, u32[]{:S(2)}) %copy-start) | copy-done | bytes 1048600
  3.1 0.0 copy-start.1
  3.2 1.2 %copy-done.1 = bf16[1,256,2048]{2,1,0:T(8,128)(2,1)S(1)} copy-done((bf16[1,256,2048]{2,1,0:T(8,128)(2,1)S(1)}, bf16[1,256,2048]{2,1,0:T(8,128)(2,1)}, u32[]{:S(2)}) %copy-start.1) | copy-done | bytes 1048600
  4.4 0.0 copy-start.2
  4.4 0.9 %copy-done.2 = bf16[1024,128]{1,0:T(8,128)(2,1)S(1)} copy-done((bf16[1024,128]{1,0:T(8,128)(2,1)S(1)}, bf16[1024,128]{1,0:T(8,128)(2,1)}, u32[]{:S(2)}) %copy-start.2) | copy-done | bytes 262168
  5.3 33.3 %shard_map.94 = (bf16[256,2048]{1,0:T(8,128)(2,1)S(1)}, bf16[256,2048]{1,0:T(8,128)(2,1)S(1)}, bf16[1024,128]{1,0:T(8,128)(2,1)S(1)}) custom-call(f32[1]{0:T(128)S(6)} %copy.13.gates_ref, s32[1]{0:T(128)S(6)} %copy.14.tiles_ref, bf16[256,2048]{1,0:T(8,128)(2,1)S(1)} %bitcast.8, bf16[1024,128]{1,0:T(8,128)(2,1)S(1)} %copy-done.2, bf16[8192,256]{1,0:T(8,128)(2,1)} %bitcast.10, ...), custom_call_target="tpu_custom_call" | custom-call | flops 2952790016 | bytes 12582912 | tf_op jit(solution)/shard_map/pallas_call | solution.py:313
  38.6 1.0 %copy.15 = bf16[1,256,2048]{2,1,0:T(8,128)(2,1)} copy(bf16[1,256,2048]{2,1,0:T(8,128)(2,1)S(1)} %bitcast.7) | data formatting | bytes 2097152
  39.6 1.0 %copy.16 = bf16[1,256,2048]{2,1,0:T(8,128)(2,1)} copy(bf16[1,256,2048]{2,1,0:T(8,128)(2,1)S(1)} %bitcast.6) | data formatting | bytes 2097152
  40.5 0.7 %copy.17 = bf16[1024,128]{1,0:T(8,128)(2,1)} copy(bf16[1024,128]{1,0:T(8,128)(2,1)S(1)} %get-tuple-element.14) | data formatting | bytes 524288
Async XLA Ops:
  1.9 1.2 %copy-start = (bf16[1,256,2048]{2,1,0:T(8,128)(2,1)S(1)}, bf16[1,256,2048]{2,1,0:T(8,128)(2,1)}, u32[]{:S(2)}) copy-start(bf16[1,256,2048]{2,1,0:T(8,128)(2,1)} %param.7) | copy-start | bytes 3145732
  3.1 1.2 %copy-start.1 = (bf16[1,256,2048]{2,1,0:T(8,128)(2,1)S(1)}, bf16[1,256,2048]{2,1,0:T(8,128)(2,1)}, u32[]{:S(2)}) copy-start(bf16[1,256,2048]{2,1,0:T(8,128)(2,1)} %param.13) | copy-start | bytes 3145732
  4.4 0.9 %copy-start.2 = (bf16[1024,128]{1,0:T(8,128)(2,1)S(1)}, bf16[1024,128]{1,0:T(8,128)(2,1)}, u32[]{:S(2)}) copy-start(bf16[1024,128]{1,0:T(8,128)(2,1)} %img_hbm.1) | copy-start | bytes 786436

commit v2 on v1

--- a/solution.py
+++ b/solution.py
@@ -35,8 +35,8 @@
 def kernel(
     n_s, n_y, block,
     gates_ref, tiles_ref, q_hbm, img_hbm, wk_hbm, wv_hbm, cot_hbm,
-    att_hbm, dq_hbm, dimg_ref,
-    wk, wv, q, cot, att, dq, img, acc, kv, dk, dv, dkv_t, probs_t, ds_t,
+    att, dq, dimg_ref,
+    w, q, cot, img, acc, kv, dk, dv, dkv_t, probs_t, ds_t,
     pair_out, pair_in, held, out_send, mid, last,
     local_sem, send_sem, img_sem, pair_sem, mid_sem, last_sem,
 ):
@@ -48,7 +48,7 @@
     chunk = img_hbm.shape[0]
     half = chunk // 2
     slots = img_hbm.shape[1]
-    width = wk.shape[1]
+    width = wk_hbm.shape[1]
     tokens, columns = q.shape
     heads = columns // HD
     group = columns // width
@@ -100,12 +100,12 @@
         pl.semaphore_signal(barrier, inc=1, device_id=device, device_id_type=MESH)
     own = bring(img_hbm, img.at[0, 0])
     parts = 4
-    depth = wk.shape[0] // parts
+    depth = w.shape[0] // parts
     weights = []
     for i in range(parts):
         piece = pl.ds(i * depth, depth)
-        weights.append(bring(wk_hbm.at[piece], wk.at[piece]))
-        weights.append(bring(wv_hbm.at[piece], wv.at[piece]))
+        weights.append(bring(wk_hbm.at[piece], w.at[piece, pl.ds(0, width)]))
+        weights.append(bring(wv_hbm.at[piece], w.at[piece, pl.ds(width, width)]))
     text = [bring(q_hbm, q), bring(cot_hbm, cot)]
     pl.semaphore_wait(barrier, len(partners))
 
@@ -132,8 +132,7 @@
     def project(ds, dy, core):
         rows = rows_of(-ds, -dy, 1 - c if core else c)
         features = img[place(ds, dy), core]
-        acc[:, :width] += dot(features, wk[rows, :], TN)
-        acc[:, width:] += dot(features, wv[rows, :], TN)
+        acc[...] += dot(features, w[rows, :], TN)
 
     for ds, dy in near_s:
         receive(ds, dy, 0, 0)
@@ -153,6 +152,12 @@
     for h in range(2):
         receive(0, 0, 1, h)
     project(0, 0, 1)
+    for copy in text:
+        copy.wait()
+    scale = jnp.tanh(jnp.full((1, HD), gates_ref[0], F32))
+    for i in range(heads):
+        part = pl.ds(i * HD, HD)
+        cot[:, part] = (scale * cot[:, part].astype(F32)).astype(BF16)
     for ds, dy in near_s:
         receive(ds, dy, 0, 1)
         share(ds, dy, 1)
@@ -178,9 +183,6 @@
     kv[...] = acc[...].astype(BF16)
     dk[...] = jnp.zeros_like(dk)
     dv[...] = jnp.zeros_like(dv)
-    for copy in text:
-        copy.wait()
-    scale = jnp.tanh(jnp.full((1, HD), gates_ref[0], F32))
     valid = tiles_ref[0] * TILE_TOK
     factor = 1.0 / math.sqrt(HD)
 
@@ -197,7 +199,7 @@
         total_v = dv[:, lanes(j)]
         for i in range(block):
             query = q[:, lanes(first + i)]
-            upstream = (scale * cot[:, lanes(first + i)].astype(F32)).astype(BF16)
+            upstream = cot[:, lanes(first + i)]
             scores = jnp.where(allowed, dot(key, query, NT) * factor, -1e30)
             expo = jnp.exp(scores - jnp.max(scores, axis=0, keepdims=True))
             probs = expo * (1.0 / jnp.sum(expo, axis=0, keepdims=True))
@@ -230,7 +232,7 @@
 
     def term(ds, dy, core):
         rows = rows_of(ds, dy, core)
-        return dot(wk[rows, :], dkv_t[:width, :], NN) + dot(wv[rows, :], dkv_t[width:, :], NN)
+        return dot(w[rows, :], dkv_t[...], NN)
 
     def start_pair(ds, dy):
         k = place(ds, dy)
@@ -264,6 +266,8 @@
         if n:
             end_pair(*order[n - 1])
     end_pair(*order[-1])
+    blocks = heads // block
+    lax.fori_loop(0, blocks // 2, finish, 0)
     for ds, dy in near_s + near_y:
         k = place(ds, dy)
         h = 1 if ds else 0
@@ -274,9 +278,7 @@
                 arrive(mid.at[h, m], mid_sem.at[h, m])
                 held[k, piece] += mid[h, m].astype(F32)
         pass_on(ds, dy, h)
-    lax.fori_loop(0, heads // block, finish, 0)
-    bring(att, att_hbm)
-    bring(dq, dq_hbm)
+    lax.fori_loop(blocks // 2, blocks, finish, 0)
     total = held[0]
     for ds, dy in near_s + near_y:
         k = place(ds, dy)
@@ -284,10 +286,17 @@
             arrive(last.at[k, pl.ds(h * half, half)], last_sem.at[k, h])
         total += last[k].astype(F32)
     dimg_ref[...] = total.astype(BF16)
-    for copy in local[-2:]:
-        copy.wait()
     for copy in sent:
         copy.wait_send()
+
+
+def write_out(count, *refs):
+    sem = refs[-1]
+    copies = [pltpu.make_async_copy(refs[i], refs[count + i], sem.at[i]) for i in range(count)]
+    for copy in copies:
+        copy.start()
+    for copy in copies:
+        copy.wait()
 
 
 def solution(mesh):
@@ -307,23 +316,20 @@
         block = math.gcd(group, 4)
         half = chunk // 2
         smem = pl.BlockSpec(memory_space=pltpu.SMEM)
-        anywhere = pl.BlockSpec(memory_space=pl.ANY)
         vmem = pl.BlockSpec(memory_space=pltpu.VMEM)
+        hbm = pl.BlockSpec(memory_space=pltpu.HBM)
         dma = pltpu.SemaphoreType.DMA
-        attended, d_query, d_image = pl.pallas_call(
+        results = pl.pallas_call(
             functools.partial(kernel, n_s, n_y, block),
             out_shape=(
-                jax.ShapeDtypeStruct((tokens, columns), BF16),
-                jax.ShapeDtypeStruct((tokens, columns), BF16),
-                jax.ShapeDtypeStruct((chunk, slots), BF16),
-            ),
-            in_specs=[smem, smem] + [anywhere] * 5,
-            out_specs=(anywhere, anywhere, vmem),
-            scratch_shapes=[
-                pltpu.VMEM((d, width), BF16),
-                pltpu.VMEM((d, width), BF16),
                 pltpu.VMEM((tokens, columns), BF16),
                 pltpu.VMEM((tokens, columns), BF16),
+                pltpu.VMEM((chunk, slots), BF16),
+            ),
+            in_specs=[smem, smem] + [hbm] * 5,
+            out_specs=(vmem, vmem, vmem),
+            scratch_shapes=[
+                pltpu.VMEM((d, 2 * width), BF16),
                 pltpu.VMEM((tokens, columns), BF16),
                 pltpu.VMEM((tokens, columns), BF16),
                 pltpu.VMEM((chips, CORES, chunk, slots), BF16),
@@ -340,7 +346,7 @@
                 pltpu.VMEM((chips, chunk, slots), BF16),
                 pltpu.VMEM((2, chips, half, slots), BF16),
                 pltpu.VMEM((chips, chunk, slots), BF16),
-                dma((13,)),
+                dma((11,)),
                 dma((counts(n_s, n_y),)),
                 dma((chips, CORES, 2)),
                 dma((chips,)),
@@ -348,7 +354,7 @@
                 dma((chips, 2)),
             ],
             compiler_params=pltpu.CompilerParams(
-                collective_id=0, has_side_effects=True, vmem_limit_bytes=48 * 1024 * 1024
+                collective_id=0, has_side_effects=True, vmem_limit_bytes=60 * 1024 * 1024
             ),
             cost_estimate=pl.CostEstimate(
                 flops=8 * d * width * slots + 12 * tokens * columns * slots,
@@ -356,6 +362,13 @@
                 transcendentals=heads * tokens * slots,
             ),
         )(gates, tiles, text, image, weight_key, weight_value, upstream)
+        attended, d_query, d_image = pl.pallas_call(
+            functools.partial(write_out, len(results)),
+            out_shape=tuple(jax.ShapeDtypeStruct(a.shape, a.dtype) for a in results),
+            in_specs=[vmem] * len(results),
+            out_specs=tuple(hbm for _ in results),
+            scratch_shapes=[dma((len(results),))],
+        )(*results)
         return attended[None], d_query[None], d_image
 
     return jax.shard_map(

time: 41.5 us -> 41.3 us (level)
  local copies, waits for them, and re-layouts: 6.04 us -> 2.67 us
  Pallas kernels: 33.3 us -> 36.5 us
    unnamed x9 -> x6, local copies, waits for them, and re-layouts: 6.04 us -> 2.67 us
    pallas_call x1 -> x2, Pallas kernels: 33.3 us -> 36.5 us  [the longest x1 33.5 us: shards(): pl.pallas_call(functools.partial(kernel, n_s, n_y, block), out_shape=(plt...]
where the time goes in v2:
time: 41.3 us; the launch traced here: 41.1 us
  Pallas kernels  36.5 us (88%)
  local copies, waits for them, and re-layouts  2.67 us (6%)
  between operations  1.94 us (5%)
    pallas_call x1, Pallas kernels, shards(): pl.pallas_call(functools.partial(kernel, n_s, n_y, block), out_shape=(plt...  33.5 us
    pallas_call x1, Pallas kernels, shards(): pl.pallas_call(functools.partial(write_out, len(results)), out_shape=tupl...  3 us
    unnamed x6, local copies, waits for them, and re-layouts  2.67 us

profile of v2, /device:TPU:0, one launch (start us, length us, event | category | flops | bytes accessed | tf_op | source)
XLA Modules:
  0.0 41.1 jit_solution(5869750567375474357)
XLA Ops:
  1.9 33.5 %shard_map.94 = (bf16[256,2048]{1,0:T(8,128)(2,1)S(1)}, bf16[256,2048]{1,0:T(8,128)(2,1)S(1)}, bf16[1024,128]{1,0:T(8,128)(2,1)S(1)}) custom-call(f32[1]{0:T(128)S(6)} %copy.10.gates_ref, s32[1]{0:T(128)S(6)} %copy.11.tiles_ref, bf16[256,2048]{1,0:T(8,128)(2,1)} %bitcast.8, bf16[1024,128]{1,0:T(8,128)(2,1)} %img_hbm.1, bf16[8192,256]{1,0:T(8,128)(2,1)} %bitcast.6, ...), custom_call_target="tpu_custom_call" | custom-call | flops 2952790016 | bytes 12582912 | tf_op jit(solution)/shard_map/pallas_call | solution.py:322
  35.4 0.0 copy-start
  35.5 1.0 %copy-done = bf16[256,2048]{1,0:T(8,128)(2,1)} copy-done((bf16[256,2048]{1,0:T(8,128)(2,1)}, bf16[256,2048]{1,0:T(8,128)(2,1)S(1)}, u32[]{:S(2)}) %copy-start) | copy-done | bytes 1048600
  36.4 0.0 copy-start.1
  36.4 1.0 %copy-done.1 = bf16[256,2048]{1,0:T(8,128)(2,1)} copy-done((bf16[256,2048]{1,0:T(8,128)(2,1)}, bf16[256,2048]{1,0:T(8,128)(2,1)S(1)}, u32[]{:S(2)}) %copy-start.1) | copy-done | bytes 1048600
  37.4 0.0 copy-start.2
  37.4 0.7 %copy-done.2 = bf16[1024,128]{1,0:T(8,128)(2,1)} copy-done((bf16[1024,128]{1,0:T(8,128)(2,1)}, bf16[1024,128]{1,0:T(8,128)(2,1)S(1)}, u32[]{:S(2)}) %copy-start.2) | copy-done | bytes 262168
  38.1 3.0 %shard_map.95 = (bf16[256,2048]{1,0:T(8,128)(2,1)}, bf16[256,2048]{1,0:T(8,128)(2,1)}, bf16[1024,128]{1,0:T(8,128)(2,1)}) custom-call(bf16[256,2048]{1,0:T(8,128)(2,1)} %copy-done, bf16[256,2048]{1,0:T(8,128)(2,1)} %copy-done.1, bf16[1024,128]{1,0:T(8,128)(2,1)} %copy-done.2), custom_call_target="tpu_custom_call" | custom-call | tf_op jit(solution)/shard_map/pallas_call | solution.py:365
Async XLA Ops:
  35.4 1.0 %copy-start = (bf16[256,2048]{1,0:T(8,128)(2,1)}, bf16[256,2048]{1,0:T(8,128)(2,1)S(1)}, u32[]{:S(2)}) copy-start(bf16[256,2048]{1,0:T(8,128)(2,1)S(1)} %get-tuple-element.9.refs_0_) | copy-start | bytes 3145732
  36.4 1.0 %copy-start.1 = (bf16[256,2048]{1,0:T(8,128)(2,1)}, bf16[256,2048]{1,0:T(8,128)(2,1)S(1)}, u32[]{:S(2)}) copy-start(bf16[256,2048]{1,0:T(8,128)(2,1)S(1)} %get-tuple-element.10.refs_1_) | copy-start | bytes 3145732
  37.4 0.7 %copy-start.2 = (bf16[1024,128]{1,0:T(8,128)(2,1)}, bf16[1024,128]{1,0:T(8,128)(2,1)S(1)}, u32[]{:S(2)}) copy-start(bf16[1024,128]{1,0:T(8,128)(2,1)S(1)} %get-tuple-element.11.refs_2_) | copy-start | bytes 786436

commit v3 on v2

--- a/solution.py
+++ b/solution.py
@@ -129,10 +129,10 @@
     def share(ds, dy, h):
         send(piece_of(ds, dy, 0, h), piece_of(ds, dy, 1, h), img_sem.at[place(ds, dy), 1, h], to(0, 0, True))
 
-    def project(ds, dy, core):
-        rows = rows_of(-ds, -dy, 1 - c if core else c)
-        features = img[place(ds, dy), core]
-        acc[...] += dot(features, w[rows, :], TN)
+    def project(ds, dy, core, first=0, length=chunk):
+        start = rows_of(-ds, -dy, 1 - c if core else c).start + first
+        features = img[place(ds, dy), core, pl.ds(first, length)]
+        acc[...] += dot(features, w[pl.ds(pl.multiple_of(start, half), length), :], TN)
 
     for ds, dy in near_s:
         receive(ds, dy, 0, 0)
@@ -174,11 +174,11 @@
         for h in range(2):
             receive(ds, dy, 0, h)
             share(ds, dy, h)
-        project(ds, dy, 0)
+            project(ds, dy, 0, h * half, half)
     for ds, dy in far:
         for h in range(2):
             receive(ds, dy, 1, h)
-        project(ds, dy, 1)
+            project(ds, dy, 1, h * half, half)
 
     kv[...] = acc[...].astype(BF16)
     dk[...] = jnp.zeros_like(dk)
@@ -215,7 +215,7 @@
         dv[:, lanes(j)] = total_v
         return carry
 
-    lax.fori_loop(0, heads // block, attend, 0)
+    lax.fori_loop(0, heads // block, attend, 0, unroll=True)
     dkv_t[:width, :] = dk[...].astype(BF16).T
     dkv_t[width:, :] = dv[...].astype(BF16).T
 
@@ -313,7 +313,7 @@
         chunk, slots = image.shape
         heads = columns // HD
         group = columns // width
-        block = math.gcd(group, 4)
+        block = math.gcd(group, 8)
         half = chunk // 2
         smem = pl.BlockSpec(memory_space=pltpu.SMEM)
         vmem = pl.BlockSpec(memory_space=pltpu.VMEM)
@@ -368,6 +368,7 @@
             in_specs=[vmem] * len(results),
             out_specs=tuple(hbm for _ in results),
             scratch_shapes=[dma((len(results),))],
+            compiler_params=pltpu.CompilerParams(vmem_limit_bytes=8 * 1024 * 1024),
         )(*results)
         return attended[None], d_query[None], d_image
 

time: 41.3 us -> 36.3 us (0.88)
  local copies, waits for them, and re-layouts: 2.67 us -> 0 us
  Pallas kernels: 36.5 us -> 34.2 us
    unnamed x6 -> x0, local copies, waits for them, and re-layouts: 2.67 us -> none
    pallas_call x1, Pallas kernels: 3 us -> 1.42 us  [shards(): pl.pallas_call(functools.partial(write_out, len(results)), out_shape=tupl...]
    pallas_call x1, Pallas kernels: 33.5 us -> 32.8 us  [shards(): pl.pallas_call(functools.partial(kernel, n_s, n_y, block), out_shape=(plt...]
where the time goes in v3:
time: 36.3 us; the launch traced here: 36.1 us
  Pallas kernels  34.2 us (94%)
  between operations  1.93 us (5%)
    pallas_call x1, Pallas kernels, shards(): pl.pallas_call(functools.partial(kernel, n_s, n_y, block), out_shape=(plt...  32.8 us
    pallas_call x1, Pallas kernels, shards(): pl.pallas_call(functools.partial(write_out, len(results)), out_shape=tupl...  1.42 us

profile of v3, /device:TPU:0, one launch (start us, length us, event | category | flops | bytes accessed | tf_op | source)
XLA Modules:
  0.0 36.1 jit_solution(17108639250188884477)
XLA Ops:
  1.9 32.8 %shard_map.94 = (bf16[256,2048]{1,0:T(8,128)(2,1)S(1)}, bf16[256,2048]{1,0:T(8,128)(2,1)S(1)}, bf16[1024,128]{1,0:T(8,128)(2,1)S(1)}) custom-call(f32[1]{0:T(128)S(6)} %copy.10.gates_ref, s32[1]{0:T(128)S(6)} %copy.11.tiles_ref, bf16[256,2048]{1,0:T(8,128)(2,1)} %bitcast.8, bf16[1024,128]{1,0:T(8,128)(2,1)} %img_hbm.1, bf16[8192,256]{1,0:T(8,128)(2,1)} %bitcast.6, ...), custom_call_target="tpu_custom_call" | custom-call | flops 2952790016 | bytes 12582912 | tf_op jit(solution)/shard_map/pallas_call | solution.py:322
  34.7 1.4 %shard_map.95 = (bf16[256,2048]{1,0:T(8,128)(2,1)}, bf16[256,2048]{1,0:T(8,128)(2,1)}, bf16[1024,128]{1,0:T(8,128)(2,1)}) custom-call(bf16[256,2048]{1,0:T(8,128)(2,1)S(1)} %get-tuple-element.9.refs_0_, bf16[256,2048]{1,0:T(8,128)(2,1)S(1)} %get-tuple-element.10.refs_1_, bf16[1024,128]{1,0:T(8,128)(2,1)S(1)} %get-tuple-element.11.refs_2_), custom_call_target="tpu_custom_call" | custom-call | tf_op jit(solution)/shard_map/pallas_call | solution.py:365

commit v4 on v3

--- a/solution.py
+++ b/solution.py
@@ -28,7 +28,7 @@
     far = (n_s - 1) * (n_y - 1)
     chips = n_s * n_y
     gather_sends = 2 * near + 2 * far + 2 * chips
-    scatter_sends = chips + 2 * far + 2 * near
+    scatter_sends = 2 * chips + 2 * far + 2 * near
     return gather_sends + scatter_sends
 
 
@@ -36,7 +36,7 @@
     n_s, n_y, block,
     gates_ref, tiles_ref, q_hbm, img_hbm, wk_hbm, wv_hbm, cot_hbm,
     att, dq, dimg_ref,
-    w, q, cot, img, acc, kv, dk, dv, dkv_t, probs_t, ds_t,
+    w, q, cot, q_t, cot_t, img, acc, kv, dk, dv, dkv_t, probs_t, ds_t,
     pair_out, pair_in, held, out_send, mid, last,
     local_sem, send_sem, img_sem, pair_sem, mid_sem, last_sem,
 ):
@@ -98,6 +98,7 @@
     partners = [to(0, 0, True)] + [to(ds, dy) for ds, dy in near_s + near_y]
     for device in partners:
         pl.semaphore_signal(barrier, inc=1, device_id=device, device_id_type=MESH)
+    text = [bring(q_hbm, q), bring(cot_hbm, cot)]
     own = bring(img_hbm, img.at[0, 0])
     parts = 4
     depth = w.shape[0] // parts
@@ -106,7 +107,6 @@
         piece = pl.ds(i * depth, depth)
         weights.append(bring(wk_hbm.at[piece], w.at[piece, pl.ds(0, width)]))
         weights.append(bring(wv_hbm.at[piece], w.at[piece, pl.ds(width, width)]))
-    text = [bring(q_hbm, q), bring(cot_hbm, cot)]
     pl.semaphore_wait(barrier, len(partners))
 
     def piece_of(ds, dy, core, h):
@@ -134,6 +134,20 @@
         features = img[place(ds, dy), core, pl.ds(first, length)]
         acc[...] += dot(features, w[pl.ds(pl.multiple_of(start, half), length), :], TN)
 
+    for copy in text:
+        copy.wait()
+    scale = jnp.tanh(jnp.full((1, HD), gates_ref[0], F32))
+    for i in range(heads):
+        part = pl.ds(i * HD, HD)
+        upstream = (scale * cot[:, part].astype(F32)).astype(BF16)
+        cot[:, part] = upstream
+        cot_t[part, :] = upstream.T
+        q_t[part, :] = q[:, part].T
+    acc[...] = jnp.zeros_like(acc)
+    for copy in weights:
+        copy.wait()
+    own.wait()
+    project(0, 0, 0)
     for ds, dy in near_s:
         receive(ds, dy, 0, 0)
         for _, ey in near_y:
@@ -144,20 +158,9 @@
         for es, _ in near_s:
             send(piece_of(0, dy, 0, 1), piece_of(es, dy, 0, 1), img_sem.at[place(es, dy), 0, 1], to(es, 0))
         share(ds, dy, 1)
-    acc[...] = jnp.zeros_like(acc)
-    for copy in weights:
-        copy.wait()
-    own.wait()
-    project(0, 0, 0)
     for h in range(2):
         receive(0, 0, 1, h)
     project(0, 0, 1)
-    for copy in text:
-        copy.wait()
-    scale = jnp.tanh(jnp.full((1, HD), gates_ref[0], F32))
-    for i in range(heads):
-        part = pl.ds(i * HD, HD)
-        cot[:, part] = (scale * cot[:, part].astype(F32)).astype(BF16)
     for ds, dy in near_s:
         receive(ds, dy, 0, 1)
         share(ds, dy, 1)
@@ -200,11 +203,11 @@
         for i in range(block):
             query = q[:, lanes(first + i)]
             upstream = cot[:, lanes(first + i)]
-            scores = jnp.where(allowed, dot(key, query, NT) * factor, -1e30)
+            scores = jnp.where(allowed, dot(key, q_t[lanes(first + i), :], NN) * factor, -1e30)
             expo = jnp.exp(scores - jnp.max(scores, axis=0, keepdims=True))
             probs = expo * (1.0 / jnp.sum(expo, axis=0, keepdims=True))
             probs_b = probs.astype(BF16)
-            d_probs = dot(value, upstream, NT)
+            d_probs = dot(value, cot_t[lanes(first + i), :], NN)
             delta = jnp.sum(probs * d_probs, axis=0, keepdims=True)
             d_scores = (probs * (d_probs - delta) * factor).astype(BF16)
             total_v += dot(probs_b, upstream, NN)
@@ -230,54 +233,54 @@
             dq[:, lanes(first + i)] = dot(ds_t[first + i], key, TN).astype(BF16)
         return carry
 
-    def term(ds, dy, core):
-        rows = rows_of(ds, dy, core)
-        return dot(w[rows, :], dkv_t[...], NN)
-
-    def start_pair(ds, dy):
-        k = place(ds, dy)
-        pair_out[k] = term(ds, dy, 1 - c).astype(BF16)
-        send(pair_out.at[k], pair_in.at[k], pair_sem.at[k], to(0, 0, True))
-        held[k] = term(ds, dy, c)
-
-    def end_pair(ds, dy):
-        k = place(ds, dy)
-        arrive(pair_in.at[k], pair_sem.at[k])
-        total = held[k] + pair_in[k].astype(F32)
-        if (ds, dy) in far:
-            out_send[k] = total.astype(BF16)
-            send(out_send.at[k, pl.ds(0, half)], mid.at[0, k], mid_sem.at[0, k], to(ds, 0))
-            send(out_send.at[k, pl.ds(half, half)], mid.at[1, k], mid_sem.at[1, k], to(0, dy))
-        else:
-            held[k] = total
-            if (ds, dy) != (0, 0):
-                h = 0 if ds else 1
-                pass_on(ds, dy, h)
-
-    def pass_on(ds, dy, h):
+    def term(ds, dy, core, h):
+        start = rows_of(ds, dy, core).start + h * half
+        return dot(w[pl.ds(pl.multiple_of(start, half), half), :], dkv_t[...], NN)
+
+    def start_pair(ds, dy, h):
         k = place(ds, dy)
         piece = pl.ds(h * half, half)
-        out_send[k, piece] = held[k, piece].astype(BF16)
-        send(out_send.at[k, piece], last.at[k, piece], last_sem.at[k, h], to(ds, dy))
-
-    order = far + near_s + near_y + [(0, 0)]
-    for n, target in enumerate(order):
-        start_pair(*target)
-        if n:
-            end_pair(*order[n - 1])
-    end_pair(*order[-1])
+        pair_out[k, piece] = term(ds, dy, 1 - c, h).astype(BF16)
+        send(pair_out.at[k, piece], pair_in.at[k, piece], pair_sem.at[k, h], to(0, 0, True))
+        held[k, piece] = term(ds, dy, c, h)
+
+    def end_pair(ds, dy, h):
+        k = place(ds, dy)
+        piece = pl.ds(h * half, half)
+        arrive(pair_in.at[k, piece], pair_sem.at[k, h])
+        total = held[k, piece] + pair_in[k, piece].astype(F32)
+        if (ds, dy) in far:
+            out_send[k, piece] = total.astype(BF16)
+            send(out_send.at[k, piece], mid.at[h, k], mid_sem.at[h, k], to(0, dy) if h else to(ds, 0))
+        elif (ds, dy, h) in direct:
+            out_send[k, piece] = total.astype(BF16)
+            send(out_send.at[k, piece], last.at[k, piece], last_sem.at[k, h], to(ds, dy))
+        else:
+            held[k, piece] = total
+
+    direct = [(ds, dy, 0) for ds, dy in near_s] + [(ds, dy, 1) for ds, dy in near_y]
+    joined = [(ds, dy, 1) for ds, dy in near_s] + [(ds, dy, 0) for ds, dy in near_y]
+    order = [(ds, dy, h) for ds, dy in far for h in range(2)] + direct + joined + [(0, 0, 0), (0, 0, 1)]
+    lag = min(3, len(order))
+    for n, unit in enumerate(order):
+        start_pair(*unit)
+        if n >= lag:
+            end_pair(*order[n - lag])
+    for unit in order[len(order) - lag:]:
+        end_pair(*unit)
     blocks = heads // block
     lax.fori_loop(0, blocks // 2, finish, 0)
-    for ds, dy in near_s + near_y:
+    for ds, dy, h in joined:
         k = place(ds, dy)
-        h = 1 if ds else 0
         piece = pl.ds(h * half, half)
+        total = held[k, piece]
         for es, ey in far:
             if (es == ds) if ds else (ey == dy):
                 m = place(es, ey)
                 arrive(mid.at[h, m], mid_sem.at[h, m])
-                held[k, piece] += mid[h, m].astype(F32)
-        pass_on(ds, dy, h)
+                total += mid[h, m].astype(F32)
+        out_send[k, piece] = total.astype(BF16)
+        send(out_send.at[k, piece], last.at[k, piece], last_sem.at[k, h], to(ds, dy))
     lax.fori_loop(blocks // 2, blocks, finish, 0)
     total = held[0]
     for ds, dy in near_s + near_y:
@@ -332,6 +335,8 @@
                 pltpu.VMEM((d, 2 * width), BF16),
                 pltpu.VMEM((tokens, columns), BF16),
                 pltpu.VMEM((tokens, columns), BF16),
+                pltpu.VMEM((columns, tokens), BF16),
+                pltpu.VMEM((columns, tokens), BF16),
                 pltpu.VMEM((chips, CORES, chunk, slots), BF16),
                 pltpu.VMEM((slots, 2 * width), F32),
                 pltpu.VMEM((slots, 2 * width), BF16),
@@ -349,7 +354,7 @@
                 dma((11,)),
                 dma((counts(n_s, n_y),)),
                 dma((chips, CORES, 2)),
-                dma((chips,)),
+                dma((chips, 2)),
                 dma((2, chips)),
                 dma((chips, 2)),
             ],

time: 36.3 us -> 36.9 us (1.017)
  Pallas kernels: 34.2 us -> 34.8 us
    pallas_call x1, Pallas kernels: 32.8 us -> 33.4 us  [shards(): pl.pallas_call(functools.partial(kernel, n_s, n_y, block), out_shape=(plt...]
where the time goes in v4:
time: 36.9 us; the launch traced here: 36.7 us
  Pallas kernels  34.8 us (94%)
  between operations  1.93 us (5%)
    pallas_call x1, Pallas kernels, shards(): pl.pallas_call(functools.partial(kernel, n_s, n_y, block), out_shape=(plt...  33.4 us
    pallas_call x1, Pallas kernels, shards(): pl.pallas_call(functools.partial(write_out, len(results)), out_shape=tupl...  1.42 us

profile of v4, /device:TPU:0, one launch (start us, length us, event | category | flops | bytes accessed | tf_op | source)
XLA Modules:
  0.0 36.7 jit_solution(13630131924948646936)
XLA Ops:
  1.9 33.4 %shard_map.94 = (bf16[256,2048]{1,0:T(8,128)(2,1)S(1)}, bf16[256,2048]{1,0:T(8,128)(2,1)S(1)}, bf16[1024,128]{1,0:T(8,128)(2,1)S(1)}) custom-call(f32[1]{0:T(128)S(6)} %copy.10.gates_ref, s32[1]{0:T(128)S(6)} %copy.11.tiles_ref, bf16[256,2048]{1,0:T(8,128)(2,1)} %bitcast.8, bf16[1024,128]{1,0:T(8,128)(2,1)} %img_hbm.1, bf16[8192,256]{1,0:T(8,128)(2,1)} %bitcast.6, ...), custom_call_target="tpu_custom_call" | custom-call | flops 2952790016 | bytes 12582912 | tf_op jit(solution)/shard_map/pallas_call | solution.py:325
  35.3 1.4 %shard_map.95 = (bf16[256,2048]{1,0:T(8,128)(2,1)}, bf16[256,2048]{1,0:T(8,128)(2,1)}, bf16[1024,128]{1,0:T(8,128)(2,1)}) custom-call(bf16[256,2048]{1,0:T(8,128)(2,1)S(1)} %get-tuple-element.9.refs_0_, bf16[256,2048]{1,0:T(8,128)(2,1)S(1)} %get-tuple-element.10.refs_1_, bf16[1024,128]{1,0:T(8,128)(2,1)S(1)} %get-tuple-element.11.refs_2_), custom_call_target="tpu_custom_call" | custom-call | tf_op jit(solution)/shard_map/pallas_call | solution.py:370

commit v5 on v4

--- a/solution.py
+++ b/solution.py
@@ -36,7 +36,7 @@
     n_s, n_y, block,
     gates_ref, tiles_ref, q_hbm, img_hbm, wk_hbm, wv_hbm, cot_hbm,
     att, dq, dimg_ref,
-    w, q, cot, q_t, cot_t, img, acc, kv, dk, dv, dkv_t, probs_t, ds_t,
+    w, q, cot, img, acc, kv, dk, dv, dkv_t, probs_t, ds_t,
     pair_out, pair_in, held, out_send, mid, last,
     local_sem, send_sem, img_sem, pair_sem, mid_sem, last_sem,
 ):
@@ -115,39 +115,34 @@
     def own_piece(h):
         return img_hbm.at[pl.ds(h * half, half)]
 
-    for h in range(2):
+    def spread(h):
         for ds, dy in near_s:
             send(own_piece(h), piece_of(ds, dy, 0, h), img_sem.at[place(ds, dy), 0, h], to(ds, dy))
         for ds, dy in near_y:
             send(own_piece(1 - h), piece_of(ds, dy, 0, 1 - h), img_sem.at[place(ds, dy), 0, 1 - h], to(ds, dy))
+
+    spread(0)
     for h in range(2):
         send(own_piece(h), piece_of(0, 0, 1, h), img_sem.at[0, 1, h], to(0, 0, True))
-
-    def receive(ds, dy, core, h):
-        arrive(piece_of(ds, dy, core, h), img_sem.at[place(ds, dy), core, h])
-
-    def share(ds, dy, h):
-        send(piece_of(ds, dy, 0, h), piece_of(ds, dy, 1, h), img_sem.at[place(ds, dy), 1, h], to(0, 0, True))
-
-    def project(ds, dy, core, first=0, length=chunk):
-        start = rows_of(-ds, -dy, 1 - c if core else c).start + first
-        features = img[place(ds, dy), core, pl.ds(first, length)]
-        acc[...] += dot(features, w[pl.ds(pl.multiple_of(start, half), length), :], TN)
-
     for copy in text:
         copy.wait()
     scale = jnp.tanh(jnp.full((1, HD), gates_ref[0], F32))
     for i in range(heads):
         part = pl.ds(i * HD, HD)
-        upstream = (scale * cot[:, part].astype(F32)).astype(BF16)
-        cot[:, part] = upstream
-        cot_t[part, :] = upstream.T
-        q_t[part, :] = q[:, part].T
-    acc[...] = jnp.zeros_like(acc)
-    for copy in weights:
-        copy.wait()
-    own.wait()
-    project(0, 0, 0)
+        cot[:, part] = (scale * cot[:, part].astype(F32)).astype(BF16)
+    spread(1)
+
+    def receive(ds, dy, core, h):
+        arrive(piece_of(ds, dy, core, h), img_sem.at[place(ds, dy), core, h])
+
+    def share(ds, dy, h):
+        send(piece_of(ds, dy, 0, h), piece_of(ds, dy, 1, h), img_sem.at[place(ds, dy), 1, h], to(0, 0, True))
+
+    def project(ds, dy, core, first=0, length=chunk):
+        start = rows_of(-ds, -dy, 1 - c if core else c).start + first
+        features = img[place(ds, dy), core, pl.ds(first, length)]
+        acc[...] += dot(features, w[pl.ds(pl.multiple_of(start, half), length), :], TN)
+
     for ds, dy in near_s:
         receive(ds, dy, 0, 0)
         for _, ey in near_y:
@@ -158,6 +153,11 @@
         for es, _ in near_s:
             send(piece_of(0, dy, 0, 1), piece_of(es, dy, 0, 1), img_sem.at[place(es, dy), 0, 1], to(es, 0))
         share(ds, dy, 1)
+    acc[...] = jnp.zeros_like(acc)
+    for copy in weights:
+        copy.wait()
+    own.wait()
+    project(0, 0, 0)
     for h in range(2):
         receive(0, 0, 1, h)
     project(0, 0, 1)
@@ -203,11 +203,11 @@
         for i in range(block):
             query = q[:, lanes(first + i)]
             upstream = cot[:, lanes(first + i)]
-            scores = jnp.where(allowed, dot(key, q_t[lanes(first + i), :], NN) * factor, -1e30)
+            scores = jnp.where(allowed, dot(key, query, NT) * factor, -1e30)
             expo = jnp.exp(scores - jnp.max(scores, axis=0, keepdims=True))
             probs = expo * (1.0 / jnp.sum(expo, axis=0, keepdims=True))
             probs_b = probs.astype(BF16)
-            d_probs = dot(value, cot_t[lanes(first + i), :], NN)
+            d_probs = dot(value, upstream, NT)
             delta = jnp.sum(probs * d_probs, axis=0, keepdims=True)
             d_scores = (probs * (d_probs - delta) * factor).astype(BF16)
             total_v += dot(probs_b, upstream, NN)
@@ -260,7 +260,7 @@
 
     direct = [(ds, dy, 0) for ds, dy in near_s] + [(ds, dy, 1) for ds, dy in near_y]
     joined = [(ds, dy, 1) for ds, dy in near_s] + [(ds, dy, 0) for ds, dy in near_y]
-    order = [(ds, dy, h) for ds, dy in far for h in range(2)] + direct + joined + [(0, 0, 0), (0, 0, 1)]
+    order = [(ds, dy, h) for ds, dy in far for h in range(2)] + joined + [(0, 0, 0), (0, 0, 1)] + direct
     lag = min(3, len(order))
     for n, unit in enumerate(order):
         start_pair(*unit)
@@ -293,9 +293,14 @@
         copy.wait_send()
 
 
-def write_out(count, *refs):
+def write_out(count, parts, *refs):
     sem = refs[-1]
-    copies = [pltpu.make_async_copy(refs[i], refs[count + i], sem.at[i]) for i in range(count)]
+    copies = []
+    for i in range(count):
+        rows = refs[i].shape[0] // parts
+        for part in range(parts):
+            piece = pl.ds(part * rows, rows)
+            copies.append(pltpu.make_async_copy(refs[i].at[piece], refs[count + i].at[piece], sem.at[i, part]))
     for copy in copies:
         copy.start()
     for copy in copies:
@@ -335,8 +340,6 @@
                 pltpu.VMEM((d, 2 * width), BF16),
                 pltpu.VMEM((tokens, columns), BF16),
                 pltpu.VMEM((tokens, columns), BF16),
-                pltpu.VMEM((columns, tokens), BF16),
-                pltpu.VMEM((columns, tokens), BF16),
                 pltpu.VMEM((chips, CORES, chunk, slots), BF16),
                 pltpu.VMEM((slots, 2 * width), F32),
                 pltpu.VMEM((slots, 2 * width), BF16),
@@ -368,11 +371,11 @@
             ),
         )(gates, tiles, text, image, weight_key, weight_value, upstream)
         attended, d_query, d_image = pl.pallas_call(
-            functools.partial(write_out, len(results)),
+            functools.partial(write_out, len(results), 4),
             out_shape=tuple(jax.ShapeDtypeStruct(a.shape, a.dtype) for a in results),
             in_specs=[vmem] * len(results),
             out_specs=tuple(hbm for _ in results),
-            scratch_shapes=[dma((len(results),))],
+            scratch_shapes=[dma((len(results), 4))],
             compiler_params=pltpu.CompilerParams(vmem_limit_bytes=8 * 1024 * 1024),
         )(*results)
         return attended[None], d_query[None], d_image

time: 36.9 us -> 37.1 us (level)
  no operation moved by 1% of the time
where the time goes in v5:
time: 37.1 us; the launch traced here: 36.9 us
  Pallas kernels  35 us (94%)
  between operations  1.93 us (5%)
    pallas_call x1, Pallas kernels, shards(): pl.pallas_call(functools.partial(kernel, n_s, n_y, block), out_shape=(plt...  33.5 us
    pallas_call x1, Pallas kernels, shards(): pl.pallas_call(functools.partial(write_out, len(results), 4), out_shape=t...  1.49 us

profile of v5, /device:TPU:0, one launch (start us, length us, event | category | flops | bytes accessed | tf_op | source)
XLA Modules:
  0.0 36.9 jit_solution(1598167825139421553)
XLA Ops:
  1.9 33.5 %shard_map.94 = (bf16[256,2048]{1,0:T(8,128)(2,1)S(1)}, bf16[256,2048]{1,0:T(8,128)(2,1)S(1)}, bf16[1024,128]{1,0:T(8,128)(2,1)S(1)}) custom-call(f32[1]{0:T(128)S(6)} %copy.10.gates_ref, s32[1]{0:T(128)S(6)} %copy.11.tiles_ref, bf16[256,2048]{1,0:T(8,128)(2,1)} %bitcast.8, bf16[1024,128]{1,0:T(8,128)(2,1)} %img_hbm.1, bf16[8192,256]{1,0:T(8,128)(2,1)} %bitcast.6, ...), custom_call_target="tpu_custom_call" | custom-call | flops 2952790016 | bytes 12582912 | tf_op jit(solution)/shard_map/pallas_call | solution.py:330
  35.5 1.5 %shard_map.95 = (bf16[256,2048]{1,0:T(8,128)(2,1)}, bf16[256,2048]{1,0:T(8,128)(2,1)}, bf16[1024,128]{1,0:T(8,128)(2,1)}) custom-call(bf16[256,2048]{1,0:T(8,128)(2,1)S(1)} %get-tuple-element.9.refs_0_, bf16[256,2048]{1,0:T(8,128)(2,1)S(1)} %get-tuple-element.10.refs_1_, bf16[1024,128]{1,0:T(8,128)(2,1)S(1)} %get-tuple-element.11.refs_2_), custom_call_target="tpu_custom_call" | custom-call | tf_op jit(solution)/shard_map/pallas_call | solution.py:373

commit v6 on v3

--- a/solution.py
+++ b/solution.py
@@ -134,6 +134,16 @@
         features = img[place(ds, dy), core, pl.ds(first, length)]
         acc[...] += dot(features, w[pl.ds(pl.multiple_of(start, half), length), :], TN)
 
+    def half_project(ds, dy, core, h):
+        project(ds, dy, core, h * half, half)
+
+    early = [(ds, dy, 0) for ds, dy in near_s] + [(ds, dy, 1) for ds, dy in near_y]
+    late = [(ds, dy, 1) for ds, dy in near_s] + [(ds, dy, 0) for ds, dy in near_y]
+    acc[...] = jnp.zeros_like(acc)
+    own.wait()
+    for copy in weights:
+        copy.wait()
+    project(0, 0, 0)
     for ds, dy in near_s:
         receive(ds, dy, 0, 0)
         for _, ey in near_y:
@@ -144,11 +154,6 @@
         for es, _ in near_s:
             send(piece_of(0, dy, 0, 1), piece_of(es, dy, 0, 1), img_sem.at[place(es, dy), 0, 1], to(es, 0))
         share(ds, dy, 1)
-    acc[...] = jnp.zeros_like(acc)
-    for copy in weights:
-        copy.wait()
-    own.wait()
-    project(0, 0, 0)
     for h in range(2):
         receive(0, 0, 1, h)
     project(0, 0, 1)
@@ -158,27 +163,33 @@
     for i in range(heads):
         part = pl.ds(i * HD, HD)
         cot[:, part] = (scale * cot[:, part].astype(F32)).astype(BF16)
-    for ds, dy in near_s:
+    for unit in early:
+        half_project(*unit[:2], 0, unit[2])
+    for unit in early:
+        receive(*unit[:2], 1, unit[2])
+        half_project(*unit[:2], 1, unit[2])
+    for unit in late:
+        receive(*unit[:2], 0, unit[2])
+        share(*unit)
+    for unit in late:
+        half_project(*unit[:2], 0, unit[2])
+    for unit in late:
+        receive(*unit[:2], 1, unit[2])
+        half_project(*unit[:2], 1, unit[2])
+    for ds, dy in far:
+        receive(ds, dy, 0, 0)
+        share(ds, dy, 0)
+        half_project(ds, dy, 0, 0)
+    for ds, dy in far:
         receive(ds, dy, 0, 1)
         share(ds, dy, 1)
-    for ds, dy in near_y:
-        receive(ds, dy, 0, 0)
-        share(ds, dy, 0)
-    for ds, dy in near_s + near_y:
-        project(ds, dy, 0)
-    for ds, dy in near_s + near_y:
-        for h in range(2):
-            receive(ds, dy, 1, h)
-        project(ds, dy, 1)
     for ds, dy in far:
-        for h in range(2):
-            receive(ds, dy, 0, h)
-            share(ds, dy, h)
-            project(ds, dy, 0, h * half, half)
+        half_project(ds, dy, 0, 1)
+        receive(ds, dy, 1, 0)
+        half_project(ds, dy, 1, 0)
     for ds, dy in far:
-        for h in range(2):
-            receive(ds, dy, 1, h)
-            project(ds, dy, 1, h * half, half)
+        receive(ds, dy, 1, 1)
+        half_project(ds, dy, 1, 1)
 
     kv[...] = acc[...].astype(BF16)
     dk[...] = jnp.zeros_like(dk)

time: 36.3 us -> 36.3 us (level)
  no operation moved by 1% of the time
where the time goes in v6:
time: 36.3 us; the launch traced here: 36.1 us
  Pallas kernels  34.2 us (94%)
  between operations  1.93 us (5%)
    pallas_call x1, Pallas kernels, shards(): pl.pallas_call(functools.partial(kernel, n_s, n_y, block), out_shape=(plt...  32.8 us
    pallas_call x1, Pallas kernels, shards(): pl.pallas_call(functools.partial(write_out, len(results)), out_shape=tupl...  1.42 us

profile of v6, /device:TPU:0, one launch (start us, length us, event | category | flops | bytes accessed | tf_op | source)
XLA Modules:
  0.0 36.1 jit_solution(17577127138923616183)
XLA Ops:
  1.9 32.8 %shard_map.94 = (bf16[256,2048]{1,0:T(8,128)(2,1)S(1)}, bf16[256,2048]{1,0:T(8,128)(2,1)S(1)}, bf16[1024,128]{1,0:T(8,128)(2,1)S(1)}) custom-call(f32[1]{0:T(128)S(6)} %copy.10.gates_ref, s32[1]{0:T(128)S(6)} %copy.11.tiles_ref, bf16[256,2048]{1,0:T(8,128)(2,1)} %bitcast.8, bf16[1024,128]{1,0:T(8,128)(2,1)} %img_hbm.1, bf16[8192,256]{1,0:T(8,128)(2,1)} %bitcast.6, ...), custom_call_target="tpu_custom_call" | custom-call | flops 2952790016 | bytes 12582912 | tf_op jit(solution)/shard_map/pallas_call | solution.py:333
  34.7 1.4 %shard_map.95 = (bf16[256,2048]{1,0:T(8,128)(2,1)}, bf16[256,2048]{1,0:T(8,128)(2,1)}, bf16[1024,128]{1,0:T(8,128)(2,1)}) custom-call(bf16[256,2048]{1,0:T(8,128)(2,1)S(1)} %get-tuple-element.9.refs_0_, bf16[256,2048]{1,0:T(8,128)(2,1)S(1)} %get-tuple-element.10.refs_1_, bf16[1024,128]{1,0:T(8,128)(2,1)S(1)} %get-tuple-element.11.refs_2_), custom_call_target="tpu_custom_call" | custom-call | tf_op jit(solution)/shard_map/pallas_call | solution.py:376
